TPU v7x, 32 devices: a whole 2x2x4 slice. The times are simulated.
32 devices in a mesh: wide: 16 (over z, y, x), narrow: 2 (over core).
Axes of the slice: x: 2, y: 2, z: 4, core: 2. Of those that a mesh axis runs over, the one named last changes fastest.
Arguments:
- right_side: bfloat16 [4, 1024, 512], P(None, 'wide'), may hold values from -6 to 6
- partial_in: float32 [2, 4, 1024, 512], P('narrow', None, 'wide'), may hold values from -6 to 6
- window_factor: bfloat16 [4, 1024, 4, 1024], P(None, 'wide', None, 'narrow'), may hold values from -0.09375 to 0.09375
- inverse_t: bfloat16 [4, 1024, 1024], P(None, 'wide', 'narrow'), as said below
- trailing_factor: bfloat16 [32768, 4, 1024], P('wide', None, 'narrow'), may hold values from -0.09375 to 0.09375
Outputs:
- solved: bfloat16 [4, 1024, 512], P(None, 'narrow')
- trailing: float32 [32768, 512], P(('wide', 'narrow'))
Inputs may be any that keep to these rules, and one draw needn't show every extreme that they name: inverse_t[k] is the transpose of the inverse of the k-th diagonal block of the lower-triangular factor: entry [k, j, i] is zero where j > i.
All inputs are finite; a program needn't handle non-finite values.
Results may differ from a plain program's by a relative error of at most 0.012.
Values may be sent and summed in bfloat16 or wider, within the bound.
A program may use at most 64 MiB of HBM per device.

v0:
```python
import jax
import jax.numpy as jnp
from jax import lax
from jax.sharding import PartitionSpec as P


def per_device(right_side, partial_in, window_factor, inverse_t, trailing_factor):
    steps_count = right_side.shape[0]
    col_width = inverse_t.shape[2]
    rhs_width = right_side.shape[2]
    trail_rows = trailing_factor.shape[0]
    solved_list = []
    for block in range(steps_count):
        fanned = partial_in[0, block]
        for prior in range(block):
            fanned = fanned + jnp.dot(
                window_factor[block, :, prior, :],
                solved_list[prior],
                preferred_element_type=jnp.float32,
            )
        fanned = lax.psum(fanned, "narrow")
        residue = (right_side[block].astype(jnp.float32) - fanned).astype(jnp.bfloat16)
        own_term = lax.dot_general(
            inverse_t[block], residue, (((0,), (0,)), ((), ())), preferred_element_type=jnp.float32
        )
        solution = lax.psum(own_term, "wide")
        solution = solution.astype(jnp.bfloat16)
        solved_list.append(solution)
    solved = jnp.stack(solved_list)
    flat_factor = trailing_factor.reshape(trail_rows, steps_count * col_width)
    flat_solved = solved.reshape(steps_count * col_width, rhs_width)
    trailing = lax.psum_scatter(
        jnp.dot(flat_factor, flat_solved, preferred_element_type=jnp.float32),
        "narrow",
        scatter_dimension=0,
        tiled=True,
    )
    return (solved, trailing)


def solution(mesh):
    placed = (
        P(None, "wide", None),
        P("narrow", None, "wide", None),
        P(None, "wide", None, "narrow"),
        P(None, "wide", "narrow"),
        P("wide", None, "narrow"),
    )
    return jax.shard_map(
        per_device,
        mesh=mesh,
        in_specs=placed,
        out_specs=(P(None, "narrow", None), P(("wide", "narrow"), None)),
        check_vma=False,
    )
```

profile of v0, /device:TPU:0, one launch (start us, length us, event | category | flops | bytes accessed | tf_op | source)
XLA Modules:
  0.0 472.1 jit_solution(9362231013797024011)
XLA Ops:
  7.2 0.0 all-reduce.9.cloned.1.call-start
  7.2 1.6 slice_bitcast_fusion
  8.8 0.0 all-reduce.9.cloned.1.call-update
  8.8 0.0 copy-start.2
  8.8 0.0 all-reduce.11.cloned.1.call-start
  8.9 2.1 fusion.38
  11.0 20.5 %all-reduce.9.cloned.1.call-done = f32[64,512]{1,0:T(8,128)} async-done(((f32[64,512]{1,0:T(8,128)}), f32[64,512]{1,0:T(8,128)}) %all-reduce.9.cloned.1.call-update) | async-done | bytes 131088 | tf_op jit(solution)/shard_map/psum | solution.py:21
  31.5 1.3 convolution_bitcast_fusion.3
  32.8 0.0 copy-start.3
  32.8 0.0 copy-start.4
  32.8 90.2 %all-reduce.16 = bf16[512,512]{0,1:T(8,128)(2,1)S(1)} all-reduce(f32[512,512]{0,1:T(8,128)S(1)} %convolution_bitcast_fusion.3), channel_id=1, replica_groups=mesh['wide'=16,'narrow'=2] {'wide'}, use_global_device_ids=true, to_apply=%region_1.0 | all-reduce | flops 262144 | bytes 1572864 | tf_op jit(solution)/shard_map/psum | solution.py:26
  123.0 0.0 copy-done.2
  123.0 0.3 fusion.9
  123.3 0.9 fusion.10
  124.3 0.0 all-reduce.11.cloned.1.call-update
  124.3 0.0 all-reduce.13.cloned.1.call-start
  124.3 0.3 fusion.7
  124.6 14.1 %all-reduce.11.cloned.1.call-done = f32[64,512]{1,0:T(8,128)} async-done(((f32[64,512]{1,0:T(8,128)}), f32[64,512]{1,0:T(8,128)}) %all-reduce.11.cloned.1.call-update) | async-done | bytes 131088 | tf_op jit(solution)/shard_map/psum | solution.py:21
  138.7 0.0 copy-done.3
  138.7 0.0 copy-done.4
  138.7 1.2 convolution_bitcast_fusion.2
  139.9 90.1 %all-reduce.17 = bf16[512,512]{0,1:T(8,128)(2,1)S(1)} all-reduce(f32[512,512]{0,1:T(8,128)S(1)} %convolution_bitcast_fusion.2), channel_id=1, replica_groups=mesh['wide'=16,'narrow'=2] {'wide'}, use_global_device_ids=true, to_apply=%region_3.0 | all-reduce | flops 262144 | bytes 1572864 | tf_op jit(solution)/shard_map/psum | solution.py:26
  230.1 0.9 fusion.8
  231.0 0.0 all-reduce.13.cloned.1.call-update
  231.0 0.0 all-reduce.15.cloned.1.call-start
  231.1 0.3 fusion.6
  231.4 14.1 %all-reduce.13.cloned.1.call-done = f32[64,512]{1,0:T(8,128)} async-done(((f32[64,512]{1,0:T(8,128)}), f32[64,512]{1,0:T(8,128)}) %all-reduce.13.cloned.1.call-update) | async-done | bytes 131088 | tf_op jit(solution)/shard_map/psum | solution.py:21
  245.5 1.2 convolution_bitcast_fusion.1
  246.7 90.1 %all-reduce.18 = bf16[512,512]{0,1:T(8,128)(2,1)S(1)} all-reduce(f32[512,512]{0,1:T(8,128)S(1)} %convolution_bitcast_fusion.1), channel_id=1, replica_groups=mesh['wide'=16,'narrow'=2] {'wide'}, use_global_device_ids=true, to_apply=%region_5.0 | all-reduce | flops 262144 | bytes 1572864 | tf_op jit(solution)/shard_map/psum | solution.py:26
  336.8 0.0 copy-start
  336.8 0.9 fusion.5
  337.8 0.0 all-reduce.15.cloned.1.call-update
  337.8 0.0 reduce-scatter.2.cloned.1.call-start
  337.9 14.3 %all-reduce.15.cloned.1.call-done = f32[64,512]{1,0:T(8,128)} async-done(((f32[64,512]{1,0:T(8,128)}), f32[64,512]{1,0:T(8,128)}) %all-reduce.15.cloned.1.call-update) | async-done | bytes 131088 | tf_op jit(solution)/shard_map/psum | solution.py:21
  352.2 1.2 convolution_bitcast_fusion
  353.4 90.2 %all-reduce.19 = bf16[512,512]{0,1:T(8,128)(2,1)S(1)} all-reduce(f32[512,512]{0,1:T(8,128)S(1)} %convolution_bitcast_fusion), channel_id=1, replica_groups=mesh['wide'=16,'narrow'=2] {'wide'}, use_global_device_ids=true, to_apply=%region_7.0 | all-reduce | flops 262144 | bytes 1572864 | tf_op jit(solution)/shard_map/psum | solution.py:26
  443.6 0.0 copy-start.1
  443.6 10.1 %fusion.2 = f32[2048,512]{0,1:T(8,128)} fusion(bf16[2048,4,512]{2,1,0:T(4,128)(2,1)} %param.9, bf16[1,512,512]{1,2,0:T(8,128)(2,1)S(1)} %bitcast.120, bf16[1,512,512]{1,2,0:T(8,128)(2,1)S(1)} %bitcast.118, bf16[1,512,512]{1,2,0:T(8,128)(2,1)S(1)} %bitcast.116, bf16[1,512,512]{1,2,0:T(8,128)(2,1)S(1)} %bitcast.114), kind=kOutput, calls=%fused_computation.2 | convolution fusion | flops 4298113024 | bytes 14680064 | tf_op jit(solution)/shard_map/dot_general | solution.py:33
  453.7 0.0 copy-done
  453.7 0.0 copy-done.1
  453.7 0.0 reduce-scatter.2.cloned.1.call-update
  453.8 1.5 pad_maximum_fusion
  455.2 2.4 copy.17
  457.6 5.1 %reduce-scatter.2.cloned.1.call-done = f32[1024,512]{0,1:T(8,128)} async-done(((f32[2048,512]{0,1:T(8,128)}), f32[1024,512]{0,1:T(8,128)}) %reduce-scatter.2.cloned.1.call-update) | async-done | bytes 2097168 | tf_op jit(solution)/shard_map/reduce_scatter | solution.py:32
  462.7 2.9 copy.18
Async XLA Ops:
  7.2 24.3 %all-reduce.9.cloned.1.call-start = ((), (), s32[]{:S(2)}) async-start(), calls=%async_computation.1 | async-start | bytes 262144 | tf_op jit(solution)/shard_map/psum | solution.py:21
  8.8 114.2 %copy-start.2 = (f32[1,4,64,512]{3,2,1,0:T(8,128)S(1)}, f32[1,4,64,512]{3,2,1,0:T(8,128)}, u32[]{:S(2)}) copy-start(f32[1,4,64,512]{3,2,1,0:T(8,128)} %param.6) | copy-start | bytes 1572868
  8.8 129.9 %all-reduce.11.cloned.1.call-start = ((), (), s32[]{:S(2)}) async-start(), calls=%async_computation.2 | async-start | bytes 262144 | tf_op jit(solution)/shard_map/psum | solution.py:21
  32.8 105.9 %copy-start.3 = (bf16[4,64,512]{2,1,0:T(8,128)(2,1)S(1)}, bf16[4,64,512]{2,1,0:T(8,128)(2,1)}, u32[]{:S(2)}) copy-start(bf16[4,64,512]{2,1,0:T(8,128)(2,1)} %param.8) | copy-start | bytes 786436
  32.8 105.9 %copy-start.4 = (bf16[4,64,512]{2,1,0:T(8,128)(2,1)S(1)}, bf16[4,64,512]{2,1,0:T(8,128)(2,1)}, u32[]{:S(2)}) copy-start(bf16[4,64,512]{2,1,0:T(8,128)(2,1)} %param.5) | copy-start | bytes 786436
  124.3 121.2 %all-reduce.13.cloned.1.call-start = ((), (), s32[]{:S(2)}) async-start(), calls=%async_computation.3 | async-start | bytes 262144 | tf_op jit(solution)/shard_map/psum | solution.py:21
  231.0 121.2 %all-reduce.15.cloned.1.call-start = ((), (), s32[]{:S(2)}) async-start(), calls=%async_computation.4 | async-start | bytes 262144 | tf_op jit(solution)/shard_map/psum | solution.py:21
  336.8 116.9 %copy-start = (bf16[512,512]{0,1:T(8,128)(2,1)}, bf16[512,512]{0,1:T(8,128)(2,1)S(1)}, u32[]{:S(2)}) copy-start(bf16[512,512]{0,1:T(8,128)(2,1)S(1)} %all-reduce.18) | copy-start | bytes 1572868
  337.8 124.9 %reduce-scatter.2.cloned.1.call-start = ((), (), s32[]{:S(2)}) async-start(), calls=%async_computation.5 | async-start | bytes 6291456 | tf_op jit(solution)/shard_map/reduce_scatter | solution.py:32
  443.6 10.1 %copy-start.1 = (bf16[512,512]{0,1:T(8,128)(2,1)}, bf16[512,512]{0,1:T(8,128)(2,1)S(1)}, u32[]{:S(2)}) copy-start(bf16[512,512]{0,1:T(8,128)(2,1)S(1)} %all-reduce.19) | copy-start | bytes 1572868
Sparse Core Ops, SparseCore 0:
  10.9 20.5 all-reduce.8
  124.4 14.2 all-reduce.10
  231.2 14.2 all-reduce.12
  337.9 14.2 all-reduce.14
  453.9 8.7 reduce-scatter.1
where the time goes:
time: 472 us
  blocking collectives  361 us (76%)
  waiting for transfers between devices  68.2 us (14%)
  matrix products  18.7 us (4%)
  between operations  13.9 us (3%)
  local copies, waits for them, and re-layouts  8.96 us (2%)
    psum x4, blocking collectives, per_device(): solution = lax.psum(own_term, 'wide')  361 us
    psum x4, waiting for transfers between devices, per_device(): fanned = lax.psum(fanned, 'narrow')  63 us
    dot_general x1, matrix products, per_device(): jnp.dot(flat_factor, flat_solved, preferred_element_type=jnp.float32)  10.1 us
  transfers between devices with their start and end apart: 5, of which 5 were waited for; matrix products, arithmetic and copies ran while one was open for 1% of the time, Pallas kernels for 0%

commit v1 on v0

v1 whole, which is shorter than its diff:
```python
import functools

import jax
import jax.numpy as jnp
from jax import lax
from jax.experimental import pallas as pl
from jax.experimental.pallas import tpu as pltpu
from jax.sharding import PartitionSpec as P

MESH = pl.DeviceIdType.MESH
INNER = 4
F32 = jnp.float32
BF16 = jnp.bfloat16


def steps_over(count, first, body):
    if count - first <= 4:
        for step in range(first, count):
            body(step)
    else:
        lax.fori_loop(first, count, lambda step, c: (body(step), c)[1], 0)


class Place:
    def __init__(self, wide, narrow):
        self.outer_count, self.narrow_count = wide // INNER, narrow
        w, n = lax.axis_index("wide"), lax.axis_index("narrow")
        self.w, self.n = w, n
        self.z, self.r = lax.div(w, INNER), lax.rem(w, INNER)
        self.c = lax.rem(n, 2)
        one = self.r + 1 - 2 * lax.rem(self.r, 2)
        two = lax.rem(self.r + 2, INNER)
        self.ra = (1 - self.c) * one + self.c * two
        self.rb = self.c * one + (1 - self.c) * two
        self.rd = INNER - 1 - self.r

    def outer(self, shift):
        return lax.rem(self.z + shift + self.outer_count, self.outer_count)

    def at(self, z, r):
        return (z * INNER + r, self.n)

    def side(self, shift):
        return lax.rem(self.n + shift + self.narrow_count, self.narrow_count)


class Gather:
    def __init__(self, place, buf, sems, k, h, peers, needed=None):
        self.p, self.buf, self.k, self.h, self.peers = place, buf, k, h, peers
        self.zs, self.zr, self.as_, self.ar, self.bs, self.br, self.ds, self.dr = sems
        self.needed = needed

    def when(self, h, z, body):
        if self.needed is None:
            body()
        else:
            pl.when(self.needed(h, z))(body)

    def copy(self, z, r, send, recv, device):
        ref = self.buf.at[self.k, self.h, z, r]
        return pltpu.make_async_remote_copy(
            src_ref=ref, dst_ref=ref, send_sem=send, recv_sem=recv, device_id=device, device_id_type=MESH
        )

    def z_copy(self, d, z, to):
        return self.copy(z, self.p.r, self.zs.at[d], self.zr.at[self.k, d], self.p.at(to, self.p.r))

    def a_copy(self, d, z, r):
        return self.copy(z, r, self.as_.at[d], self.ar.at[self.k, d], self.p.at(self.p.z, self.p.ra))

    def b_copy(self, d, which, z, r):
        return self.copy(z, r, self.bs.at[which, d], self.br.at[self.k, which, d], self.p.at(self.p.z, self.p.rb))

    def d_copy(self, d, i, z, h, to):
        ref = self.buf.at[self.k, h, z]
        return pltpu.make_async_remote_copy(
            src_ref=ref, dst_ref=ref, send_sem=self.ds.at[i, d], recv_sem=self.dr.at[self.k, i, d],
            device_id=(self.p.w, to), device_id_type=MESH,
        )

    def own(self):
        p = self.p

        def go():
            steps_over(p.outer_count, 1, lambda d: self.z_copy(d, p.z, p.outer(d)).start())
            self.a_copy(0, p.z, p.r).start()
            self.b_copy(0, 0, p.z, p.r).start()

        self.when(self.h, p.z, go)

    def line(self):
        p = self.p

        def one(d):
            z = p.outer(-d)

            def go():
                self.z_copy(d, z, p.z).wait_recv()
                self.a_copy(d, z, p.r).start()
                self.b_copy(d, 0, z, p.r).start()

            self.when(self.h, z, go)

        steps_over(p.outer_count, 1, one)

    def first_side(self):
        p = self.p

        def one(d):
            z = p.outer(-d)

            def go():
                self.a_copy(d, z, p.ra).wait_recv()
                self.b_copy(d, 1, z, p.ra).start()

            self.when(self.h, z, go)

        steps_over(p.outer_count, 0, one)

    def second_side(self):
        p = self.p

        def one(d):
            z = p.outer(-d)

            def go():
                self.b_copy(d, 0, z, p.rb).wait_recv()
                self.b_copy(d, 1, z, p.rd).wait_recv()
                for i, (to, _) in enumerate(self.peers):
                    self.d_copy(d, i, z, self.h, to).start()

            self.when(self.h, z, go)

        steps_over(p.outer_count, 0, one)

    def across(self):
        p = self.p
        for i, (_, source) in enumerate(self.peers):

            def one(d, i=i, source=source):
                z = p.outer(-d)
                self.when(source, z, lambda: self.d_copy(d, i, z, source, p.n).wait_recv())

            steps_over(p.outer_count, 0, one)

    def sent(self):
        p = self.p
        self.when(
            self.h, p.z,
            lambda: steps_over(p.outer_count, 1, lambda d: self.z_copy(d, p.z, p.outer(d)).wait_send()),
        )

        def one(d):
            z = p.outer(-d)

            def go():
                self.a_copy(d, z, p.r).wait_send()
                self.b_copy(d, 0, z, p.r).wait_send()
                self.b_copy(d, 1, z, p.ra).wait_send()
                for i, (to, _) in enumerate(self.peers):
                    self.d_copy(d, i, z, self.h, to).wait_send()

            self.when(self.h, z, go)

        steps_over(p.outer_count, 0, one)


def kernel(
    wide, narrow, right, partial, window, inverse, factor, solved, trailing,
    ybuf, ibuf, xbuf, tbuf, pbuf, wbuf, fan,
    y_zs, y_zr, y_as, y_ar, y_bs, y_br, y_ds, y_dr,
    i_zs, i_zr, i_as, i_ar, i_bs, i_br, i_ds, i_dr,
    p_s, p_r, w_s, w_r, t_s, t_r, t_own,
):
    place = Place(wide, narrow)
    n = place.n
    blocks, rows, rhs = right.shape
    cols = inverse.shape[2]
    half = rhs // 2
    step_rows = wide * rows
    outer_rows = INNER * rows
    trail = trailing.shape[0]
    shifts = range(1, narrow)

    barrier = pltpu.get_barrier_semaphore()

    def greet(device):
        pl.semaphore_signal(barrier, inc=1, device_id=device, device_id_type=MESH)

    steps_over(place.outer_count, 1, lambda d: greet(place.at(place.outer(d), place.r)))
    greet(place.at(place.z, place.ra))
    greet(place.at(place.z, place.rb))
    for s in shifts:
        greet((place.w, place.side(s)))
    pl.semaphore_wait(barrier, place.outer_count - 1 + 2 + narrow - 1)

    def side_copy(src, dst, send, recv, s):
        return pltpu.make_async_remote_copy(
            src_ref=src, dst_ref=dst, send_sem=send, recv_sem=recv,
            device_id=(place.w, place.side(s)), device_id_type=MESH,
        )

    def p_copy(s, k):
        return side_copy(partial.at[0, k], pbuf.at[s - 1, k], p_s.at[s - 1, k], p_r.at[s - 1, k], s)

    def w_copy(s, slot):
        return side_copy(window, wbuf.at[slot], w_s.at[s - 1], w_r.at[s - 1], s)

    def t_copy(s, slot):
        to = place.side(s)
        return side_copy(
            factor.at[:, pl.ds(pl.multiple_of(to * trail, trail), trail), :], tbuf.at[slot],
            t_s.at[s - 1], t_r.at[s - 1], s,
        )

    t_here = pltpu.make_async_copy(
        factor.at[:, pl.ds(pl.multiple_of(n * trail, trail), trail), :], tbuf.at[n], t_own
    )

    for s in shifts:
        p_copy(s, 0).start()

    mate = n + 1 - 2 * place.c
    y_sems = (y_zs, y_zr, y_as, y_ar, y_bs, y_br, y_ds, y_dr)
    i_sems = (i_zs, i_zr, i_as, i_ar, i_bs, i_br, i_ds, i_dr)
    everyone = [(place.side(s), place.side(-s)) for s in shifts]
    ys = [Gather(place, ybuf, y_sems, k, place.c, [(mate, 1 - place.c)]) for k in range(blocks)]
    needed = lambda h, z: z * outer_rows < (h + 1) * cols
    inv = [Gather(place, ibuf, i_sems, k, n, everyone, needed) for k in range(blocks)]

    ibuf[0, n, place.z, place.r] = inverse[0]
    inv[0].own()

    def residue(k):
        fanned = partial[0, k]
        for s in shifts:
            fanned = fanned + pbuf[s - 1, k]
        if k > 0:
            fanned = fanned + fan[...]
        value = (right[k].astype(F32) - fanned).astype(BF16)
        for c in range(2):

            @pl.when(place.c == c)
            def _():
                ybuf[k, c, place.z, place.r] = value[:, c * half:(c + 1) * half]

    for s in shifts:
        p_copy(s, 0).wait_recv()
    residue(0)
    ys[0].own()

    for s in shifts:
        for k in range(1, blocks):
            p_copy(s, k).start()
        w_copy(s, n).start()
        t_copy(s, n).start()
    t_here.start()
    for k in range(1, blocks):
        ibuf[k, n, place.z, place.r] = inverse[k]
    wbuf[n] = window[...]

    width = min(256, cols)

    def solve(k):
        for h in range(narrow):
            deep = min(place.outer_count, -(-(h + 1) * cols // outer_rows))

            def tile(t, h=h, deep=deep):
                at = pl.multiple_of(t * width, width)
                lhs = ibuf[k, h, :deep, :, :, pl.ds(at, width)].reshape(deep * outer_rows, width)
                for c in range(2):
                    rhs_part = ybuf[k, c, :deep].reshape(deep * outer_rows, half)
                    out = lax.dot_general(lhs, rhs_part, (((0,), (0,)), ((), ())), preferred_element_type=F32)
                    xbuf[k, pl.ds(pl.multiple_of(h * cols + at, width), width), c * half:(c + 1) * half] = out.astype(BF16)

            lax.fori_loop(0, cols // width, lambda t, carry: (tile(t), carry)[1], 0)

    def fan_in(k, j):
        total = None
        for h in range(narrow):
            term = jnp.dot(
                wbuf[h, k * (k - 1) // 2 + j], xbuf[j, h * cols:(h + 1) * cols, :], preferred_element_type=F32
            )
            total = term if total is None else total + term
        if j == 0:
            fan[...] = total
        else:
            fan[...] += total

    high = min(256, trail)

    def trail_in(k):
        def tile(t):
            at = pl.ds(pl.multiple_of(t * high, high), high)
            total = None
            for h in range(narrow):
                term = jnp.dot(tbuf[h, k, at, :], xbuf[k, h * cols:(h + 1) * cols, :], preferred_element_type=F32)
                total = term if total is None else total + term
            if k == 0:
                trailing[at, :] = total
            else:
                trailing[at, :] += total

        lax.fori_loop(0, trail // high, lambda t, carry: (tile(t), carry)[1], 0)

    inv[0].line()
    ys[0].line()
    for k in range(blocks):
        y, last = ys[k], k == blocks - 1
        if k > 0:
            y.line()
        y.first_side()
        if k == 0:
            inv[0].first_side()
        if not last:
            if k > 0:
                inv[k].sent()
        if k == 0:
            inv[0].second_side()
            inv[0].sent()
        if not last:
            inv[k + 1].own()
        if k == 1:
            for s in shifts:
                t_copy(s, place.side(-s)).wait_recv()
            t_here.wait()
        if k > 0:
            trail_in(k - 1)
            if not last:
                for j in range(k):
                    fan_in(k + 1, j)
        y.second_side()
        if not last:
            inv[k + 1].line()
        inv[k].across()
        y.across()
        solve(k)
        y.sent()
        if not last:
            if k == 0:
                for s in shifts:
                    w_copy(s, place.side(-s)).wait_recv()
                    for later in range(1, blocks):
                        p_copy(s, later).wait_recv()
            fan_in(k + 1, k)
            residue(k + 1)
            ys[k + 1].own()
            inv[k + 1].first_side()
            inv[k + 1].second_side()
    inv[blocks - 1].sent()
    trail_in(blocks - 1)
    for h in range(narrow):

        @pl.when(n == h)
        def _():
            for k in range(blocks):
                solved[k] = xbuf[k, h * cols:(h + 1) * cols, :]

    for s in shifts:
        for k in range(blocks):
            p_copy(s, k).wait_send()
        w_copy(s, n).wait_send()
        t_copy(s, n).wait_send()


def per_device(wide, narrow, right_side, partial_in, window_factor, inverse_t, trailing_factor):
    blocks, rows, rhs = right_side.shape
    cols = inverse_t.shape[2]
    trail = trailing_factor.shape[0] // narrow
    outer = wide // INNER
    window = jnp.stack([window_factor[k, :, j, :] for k in range(blocks) for j in range(k)])
    factor = jnp.transpose(trailing_factor, (1, 0, 2))
    dma = pltpu.SemaphoreType.DMA

    def gather_sems(peers):
        return [
            dma((outer,)), dma((blocks, outer)),
            dma((outer,)), dma((blocks, outer)),
            dma((2, outer)), dma((blocks, 2, outer)),
            dma((peers, outer)), dma((blocks, peers, outer)),
        ]

    vmem = pl.BlockSpec(memory_space=pltpu.VMEM)
    step_rows = wide * rows
    return pl.pallas_call(
        functools.partial(kernel, wide, narrow),
        out_shape=(
            jax.ShapeDtypeStruct((blocks, cols, rhs), BF16),
            jax.ShapeDtypeStruct((trail, rhs), F32),
        ),
        in_specs=[vmem, vmem, vmem, vmem, pl.BlockSpec(memory_space=pl.ANY)],
        out_specs=(vmem, vmem),
        scratch_shapes=[
            pltpu.VMEM((blocks, 2, outer, INNER, rows, rhs // 2), BF16),
            pltpu.VMEM((blocks, narrow, outer, INNER, rows, cols), BF16),
            pltpu.VMEM((blocks, step_rows, rhs), BF16),
            pltpu.VMEM((narrow, blocks, trail, cols), BF16),
            pltpu.VMEM((narrow - 1, blocks, rows, rhs), F32),
            pltpu.VMEM((narrow, blocks * (blocks - 1) // 2, rows, cols), BF16),
            pltpu.VMEM((rows, rhs), F32),
            *gather_sems(1),
            *gather_sems(narrow - 1),
            dma((narrow - 1, blocks)), dma((narrow - 1, blocks)),
            dma((narrow - 1,)), dma((narrow - 1,)),
            dma((narrow - 1,)), dma((narrow - 1,)),
            dma,
        ],
        compiler_params=pltpu.CompilerParams(
            collective_id=0, has_side_effects=True, vmem_limit_bytes=56 * 1024 * 1024
        ),
    )(right_side, partial_in, window, inverse_t, factor)


def solution(mesh):
    placed = (
        P(None, "wide", None),
        P("narrow", None, "wide", None),
        P(None, "wide", None, "narrow"),
        P(None, "wide", "narrow"),
        P("wide", None, "narrow"),
    )
    return jax.shard_map(
        functools.partial(per_device, mesh.shape["wide"], mesh.shape["narrow"]),
        mesh=mesh,
        in_specs=placed,
        out_specs=(P(None, "narrow", None), P(("wide", "narrow"), None)),
        check_vma=False,
    )
```

time: 472 us -> 102 us (0.22)
  blocking collectives: 361 us -> 0 us
  Pallas kernels: 0 us -> 85.8 us
  waiting for transfers between devices: 68.2 us -> 0 us
  matrix products: 18.7 us -> 0 us
  between operations: 13.9 us -> 0.71 us
  local copies, waits for them, and re-layouts: 8.96 us -> 15.1 us
    psum x4 -> x0, blocking collectives: 361 us -> none  [per_device(): solution = lax.psum(own_term, 'wide')]
    pallas_call x0 -> x1, Pallas kernels: none -> 85.8 us  [per_device(): pl.pallas_call(functools.partial(kernel, wide, narrow), out_shape=(jax.Sh...]
    psum x4 -> x0, waiting for transfers between devices: 63 us -> none  [per_device(): fanned = lax.psum(fanned, 'narrow')]
    dot_general x11 -> x0, matrix products: 18.7 us -> none  [the longest x1 10.1 us: per_device(): jnp.dot(flat_factor, flat_solved, preferred_element_type=jnp.float32)]
    unnamed x12, local copies, waits for them, and re-layouts: 5.27 us -> 13 us
    reduce_scatter x1 -> x0, waiting for transfers between devices: 5.06 us -> none  [per_device(): lax.psum_scatter(jnp.dot(flat_factor, flat_solved, preferred_element_type...]
  transfers between devices with their start and end apart: 5 -> 0, of which waited for: 5 -> 0; matrix products, arithmetic and copies ran while one was open for 1% -> 0% of each run, Pallas kernels for 0% -> 0%
where the time goes in v1:
time: 102 us
  Pallas kernels  85.8 us (84%)
  local copies, waits for them, and re-layouts  15.1 us (15%)
    pallas_call x1, Pallas kernels, per_device(): pl.pallas_call(functools.partial(kernel, wide, narrow), out_shape=(jax.Sh...  85.8 us
    unnamed x12, local copies, waits for them, and re-layouts  13 us
    slice x1, local copies, waits for them, and re-layouts, per_device(): window_factor[k, :, j, :]  2.11 us

profile of v1, /device:TPU:0, one launch (start us, length us, event | category | flops | bytes accessed | tf_op | source)
XLA Modules:
  0.0 101.6 jit_solution(10504463509918396312)
XLA Ops:
  0.6 2.1 %fusion.6 = (bf16[1,64,1,512]{3,2,1,0:T(2,128)(2,1)S(1)}, bf16[1,64,1,512]{3,2,1,0:T(2,128)(2,1)S(1)}, bf16[1,64,1,512]{3,2,1,0:T(2,128)(2,1)S(1)}, bf16[1,64,1,...) fusion(bf16[4,64,4,512]{3,2,1,0:T(4,128)(2,1)} %param.7), kind=kLoop, calls=%fused_computation.13 | loop fusion | bytes 786432 | tf_op jit(solution)/shard_map/slice | solution.py:371
  2.9 0.0 copy-start.1
  2.9 8.4 %copy.39 = bf16[2048,4,512]{2,0,1:T(8,128)(2,1)} copy(bf16[2048,4,512]{2,1,0:T(4,128)(2,1)} %param.9) | data formatting | bytes 16777216 | tf_op args[4]
  11.3 0.0 copy-done.1
  11.3 85.8 %shard_map.68 = (bf16[4,512,512]{2,1,0:T(8,128)(2,1)}, f32[1024,512]{1,0:T(8,128)}) custom-call(bf16[4,64,512]{2,1,0:T(8,128)(2,1)} %right.1, f32[1,4,64,512]{3,2,1,0:T(8,128)} %partial.1, bf16[6,64,512]{2,1,0:T(8,128)(2,1)} %copy-done.1, bf16[4,64,512]{2,1,0:T(8,128)(2,1)} %inverse.1, bf16[4,2048,512]{2,1,0:T(8,128)(2,1)} %bitcast.27), custom_call_target="tpu_custom_call" | custom-call | tf_op jit(solution)/shard_map/pallas_call | solution.py:385
  97.1 0.0 copy-start
  97.1 3.2 %copy.47 = bf16[4,512,512]{2,1,0:T(8,128)(2,1)} copy(bf16[4,512,512]{2,1,0:T(8,128)(2,1)} %get-tuple-element.10) | data formatting | bytes 4194304
  100.3 0.0 copy-done
  100.3 1.3 %copy.48 = f32[1024,512]{1,0:T(8,128)} copy(f32[1024,512]{1,0:T(8,128)S(1)} %copy-done) | data formatting | bytes 4194304
  (6 shorter events, 0.1 us)
Async XLA Ops:
  2.9 8.5 %copy-start.1 = (bf16[6,64,512]{2,1,0:T(8,128)(2,1)}, bf16[6,64,512]{2,1,0:T(8,128)(2,1)S(1)}, u32[]{:S(2)}) copy-start(bf16[6,64,512]{2,1,0:T(8,128)(2,1)S(1)} %fusion.window) | copy-start | bytes 1179652
  97.1 3.2 %copy-start = (f32[1024,512]{1,0:T(8,128)S(1)}, f32[1024,512]{1,0:T(8,128)}, u32[]{:S(2)}) copy-start(f32[1024,512]{1,0:T(8,128)} %get-tuple-element.11) | copy-start | bytes 6291460

commit v2 on v1

--- a/solution.py
+++ b/solution.py
@@ -63,18 +63,18 @@
         )
 
     def z_copy(self, d, z, to):
-        return self.copy(z, self.p.r, self.zs.at[d], self.zr.at[self.k, d], self.p.at(to, self.p.r))
+        return self.copy(z, self.p.r, self.zs.at[self.k % 2, d], self.zr.at[self.k, d], self.p.at(to, self.p.r))
 
     def a_copy(self, d, z, r):
-        return self.copy(z, r, self.as_.at[d], self.ar.at[self.k, d], self.p.at(self.p.z, self.p.ra))
+        return self.copy(z, r, self.as_.at[self.k % 2, d], self.ar.at[self.k, d], self.p.at(self.p.z, self.p.ra))
 
     def b_copy(self, d, which, z, r):
-        return self.copy(z, r, self.bs.at[which, d], self.br.at[self.k, which, d], self.p.at(self.p.z, self.p.rb))
+        return self.copy(z, r, self.bs.at[self.k % 2, which, d], self.br.at[self.k, which, d], self.p.at(self.p.z, self.p.rb))
 
     def d_copy(self, d, i, z, h, to):
         ref = self.buf.at[self.k, h, z]
         return pltpu.make_async_remote_copy(
-            src_ref=ref, dst_ref=ref, send_sem=self.ds.at[i, d], recv_sem=self.dr.at[self.k, i, d],
+            src_ref=ref, dst_ref=ref, send_sem=self.ds.at[self.k % 2, i, d], recv_sem=self.dr.at[self.k, i, d],
             device_id=(self.p.w, to), device_id_type=MESH,
         )
 
@@ -303,23 +303,25 @@
 
         lax.fori_loop(0, trail // high, lambda t, carry: (tile(t), carry)[1], 0)
 
+    if blocks > 1:
+        inv[1].own()
     inv[0].line()
     ys[0].line()
+    inv[0].first_side()
     for k in range(blocks):
         y, last = ys[k], k == blocks - 1
         if k > 0:
             y.line()
         y.first_side()
         if k == 0:
-            inv[0].first_side()
+            inv[0].second_side()
+            if not last:
+                inv[1].line()
         if not last:
-            if k > 0:
-                inv[k].sent()
-        if k == 0:
-            inv[0].second_side()
-            inv[0].sent()
-        if not last:
-            inv[k + 1].own()
+            inv[k + 1].first_side()
+        if k + 2 < blocks:
+            inv[k].sent()
+            inv[k + 2].own()
         if k == 1:
             for s in shifts:
                 t_copy(s, place.side(-s)).wait_recv()
@@ -330,8 +332,6 @@
                 for j in range(k):
                     fan_in(k + 1, j)
         y.second_side()
-        if not last:
-            inv[k + 1].line()
         inv[k].across()
         y.across()
         solve(k)
@@ -345,9 +345,11 @@
             fan_in(k + 1, k)
             residue(k + 1)
             ys[k + 1].own()
-            inv[k + 1].first_side()
             inv[k + 1].second_side()
-    inv[blocks - 1].sent()
+        if k + 2 < blocks:
+            inv[k + 2].line()
+    for k in range(max(0, blocks - 2), blocks):
+        inv[k].sent()
     trail_in(blocks - 1)
     for h in range(narrow):
 
@@ -374,10 +376,10 @@
 
     def gather_sems(peers):
         return [
-            dma((outer,)), dma((blocks, outer)),
-            dma((outer,)), dma((blocks, outer)),
-            dma((2, outer)), dma((blocks, 2, outer)),
-            dma((peers, outer)), dma((blocks, peers, outer)),
+            dma((2, outer)), dma((blocks, outer)),
+            dma((2, outer)), dma((blocks, outer)),
+            dma((2, 2, outer)), dma((blocks, 2, outer)),
+            dma((2, peers, outer)), dma((blocks, peers, outer)),
         ]
 
     vmem = pl.BlockSpec(memory_space=pltpu.VMEM)

time: 102 us -> 99.1 us (0.972)
  Pallas kernels: 85.8 us -> 82.2 us
    pallas_call x1, Pallas kernels: 85.8 us -> 82.2 us  [per_device(): pl.pallas_call(functools.partial(kernel, wide, narrow), out_shape=(jax.Sh...]
where the time goes in v2:
time: 99.1 us; the launch traced here: 98 us
  Pallas kernels  82.2 us (83%)
  local copies, waits for them, and re-layouts  15.1 us (15%)
    pallas_call x1, Pallas kernels, per_device(): pl.pallas_call(functools.partial(kernel, wide, narrow), out_shape=(jax.Sh...  82.2 us
    unnamed x12, local copies, waits for them, and re-layouts  13 us
    slice x1, local copies, waits for them, and re-layouts, per_device(): window_factor[k, :, j, :]  2.11 us

profile of v2, /device:TPU:0, one launch (start us, length us, event | category | flops | bytes accessed | tf_op | source)
XLA Modules:
  0.0 98.0 jit_solution(5606908611625991603)
XLA Ops:
  0.6 2.1 %fusion.6 = (bf16[1,64,1,512]{3,2,1,0:T(2,128)(2,1)S(1)}, bf16[1,64,1,512]{3,2,1,0:T(2,128)(2,1)S(1)}, bf16[1,64,1,512]{3,2,1,0:T(2,128)(2,1)S(1)}, bf16[1,64,1,...) fusion(bf16[4,64,4,512]{3,2,1,0:T(4,128)(2,1)} %param.7), kind=kLoop, calls=%fused_computation.13 | loop fusion | bytes 786432 | tf_op jit(solution)/shard_map/slice | solution.py:373
  2.9 0.0 copy-start.1
  2.9 8.4 %copy.39 = bf16[2048,4,512]{2,0,1:T(8,128)(2,1)} copy(bf16[2048,4,512]{2,1,0:T(4,128)(2,1)} %param.9) | data formatting | bytes 16777216 | tf_op args[4]
  11.3 0.0 copy-done.1
  11.3 82.2 %shard_map.68 = (bf16[4,512,512]{2,1,0:T(8,128)(2,1)}, f32[1024,512]{1,0:T(8,128)}) custom-call(bf16[4,64,512]{2,1,0:T(8,128)(2,1)} %right.1, f32[1,4,64,512]{3,2,1,0:T(8,128)} %partial.1, bf16[6,64,512]{2,1,0:T(8,128)(2,1)} %copy-done.1, bf16[4,64,512]{2,1,0:T(8,128)(2,1)} %inverse.1, bf16[4,2048,512]{2,1,0:T(8,128)(2,1)} %bitcast.27), custom_call_target="tpu_custom_call" | custom-call | tf_op jit(solution)/shard_map/pallas_call | solution.py:387
  93.5 0.0 copy-start
  93.5 3.2 %copy.47 = bf16[4,512,512]{2,1,0:T(8,128)(2,1)} copy(bf16[4,512,512]{2,1,0:T(8,128)(2,1)} %get-tuple-element.10) | data formatting | bytes 4194304
  96.7 0.0 copy-done
  96.7 1.3 %copy.48 = f32[1024,512]{1,0:T(8,128)} copy(f32[1024,512]{1,0:T(8,128)S(1)} %copy-done) | data formatting | bytes 4194304
  (6 shorter events, 0.1 us)
Async XLA Ops:
  2.9 8.5 %copy-start.1 = (bf16[6,64,512]{2,1,0:T(8,128)(2,1)}, bf16[6,64,512]{2,1,0:T(8,128)(2,1)S(1)}, u32[]{:S(2)}) copy-start(bf16[6,64,512]{2,1,0:T(8,128)(2,1)S(1)} %fusion.window) | copy-start | bytes 1179652
  93.5 3.2 %copy-start = (f32[1024,512]{1,0:T(8,128)S(1)}, f32[1024,512]{1,0:T(8,128)}, u32[]{:S(2)}) copy-start(f32[1024,512]{1,0:T(8,128)} %get-tuple-element.11) | copy-start | bytes 6291460

commit v3 on v2

--- a/solution.py
+++ b/solution.py
@@ -167,7 +167,7 @@
 
 def kernel(
     wide, narrow, right, partial, window, inverse, factor, solved, trailing,
-    ybuf, ibuf, xbuf, tbuf, pbuf, wbuf, fan,
+    ybuf, ibuf, xbuf, tbuf, pbuf, wbuf, fan, turned,
     y_zs, y_zr, y_as, y_ar, y_bs, y_br, y_ds, y_dr,
     i_zs, i_zr, i_as, i_ar, i_bs, i_br, i_ds, i_dr,
     p_s, p_r, w_s, w_r, t_s, t_r, t_own,
@@ -206,11 +206,11 @@
     def w_copy(s, slot):
         return side_copy(window, wbuf.at[slot], w_s.at[s - 1], w_r.at[s - 1], s)
 
-    def t_copy(s, slot):
+    def t_copy(s, slot, k):
         to = place.side(s)
         return side_copy(
-            factor.at[:, pl.ds(pl.multiple_of(to * trail, trail), trail), :], tbuf.at[slot],
-            t_s.at[s - 1], t_r.at[s - 1], s,
+            factor.at[k, pl.ds(pl.multiple_of(to * trail, trail), trail), :], tbuf.at[slot, k],
+            t_s.at[s - 1, k], t_r.at[s - 1, k], s,
         )
 
     t_here = pltpu.make_async_copy(
@@ -253,7 +253,6 @@
         for k in range(1, blocks):
             p_copy(s, k).start()
         w_copy(s, n).start()
-        t_copy(s, n).start()
     t_here.start()
     for k in range(1, blocks):
         ibuf[k, n, place.z, place.r] = inverse[k]
@@ -261,17 +260,26 @@
 
     width = min(256, cols)
 
+    def turn(k):
+        inv[k].across()
+        for h in range(narrow):
+            deep = min(place.outer_count, -(-(h + 1) * cols // outer_rows))
+            for q in range(deep):
+                for t in range(cols // width):
+                    block = ibuf[k, h, q, :, :, t * width:(t + 1) * width].reshape(outer_rows, width)
+                    turned[h * cols + t * width:h * cols + (t + 1) * width, q * outer_rows:(q + 1) * outer_rows] = block.T
+
     def solve(k):
         for h in range(narrow):
             deep = min(place.outer_count, -(-(h + 1) * cols // outer_rows))
 
             def tile(t, h=h, deep=deep):
-                at = pl.multiple_of(t * width, width)
-                lhs = ibuf[k, h, :deep, :, :, pl.ds(at, width)].reshape(deep * outer_rows, width)
+                at = pl.ds(pl.multiple_of(h * cols + t * width, width), width)
+                lhs = turned[at, :deep * outer_rows]
                 for c in range(2):
                     rhs_part = ybuf[k, c, :deep].reshape(deep * outer_rows, half)
-                    out = lax.dot_general(lhs, rhs_part, (((0,), (0,)), ((), ())), preferred_element_type=F32)
-                    xbuf[k, pl.ds(pl.multiple_of(h * cols + at, width), width), c * half:(c + 1) * half] = out.astype(BF16)
+                    out = jnp.dot(lhs, rhs_part, preferred_element_type=F32)
+                    xbuf[k, at, c * half:(c + 1) * half] = out.astype(BF16)
 
             lax.fori_loop(0, cols // width, lambda t, carry: (tile(t), carry)[1], 0)
 
@@ -303,6 +311,7 @@
 
         lax.fori_loop(0, trail // high, lambda t, carry: (tile(t), carry)[1], 0)
 
+    sending = [[k, k + 1] if k == 1 else [k + (k > 1)] if k + (k > 1) < blocks else [] for k in range(blocks)]
     if blocks > 1:
         inv[1].own()
     inv[0].line()
@@ -323,17 +332,23 @@
             inv[k].sent()
             inv[k + 2].own()
         if k == 1:
-            for s in shifts:
-                t_copy(s, place.side(-s)).wait_recv()
             t_here.wait()
         if k > 0:
+            for s in shifts:
+                t_copy(s, place.side(-s), k - 1).wait_recv()
             trail_in(k - 1)
             if not last:
                 for j in range(k):
                     fan_in(k + 1, j)
+        if k > 0:
+            turn(k)
         y.second_side()
-        inv[k].across()
+        if k == 0:
+            turn(k)
         y.across()
+        for part in sending[k]:
+            for s in shifts:
+                t_copy(s, n, part).start()
         solve(k)
         y.sent()
         if not last:
@@ -350,6 +365,8 @@
             inv[k + 2].line()
     for k in range(max(0, blocks - 2), blocks):
         inv[k].sent()
+    for s in shifts:
+        t_copy(s, place.side(-s), blocks - 1).wait_recv()
     trail_in(blocks - 1)
     for h in range(narrow):
 
@@ -362,7 +379,8 @@
         for k in range(blocks):
             p_copy(s, k).wait_send()
         w_copy(s, n).wait_send()
-        t_copy(s, n).wait_send()
+        for k in range(blocks):
+            t_copy(s, n, k).wait_send()
 
 
 def per_device(wide, narrow, right_side, partial_in, window_factor, inverse_t, trailing_factor):
@@ -400,11 +418,12 @@
             pltpu.VMEM((narrow - 1, blocks, rows, rhs), F32),
             pltpu.VMEM((narrow, blocks * (blocks - 1) // 2, rows, cols), BF16),
             pltpu.VMEM((rows, rhs), F32),
+            pltpu.VMEM((step_rows, step_rows), BF16),
             *gather_sems(1),
             *gather_sems(narrow - 1),
             dma((narrow - 1, blocks)), dma((narrow - 1, blocks)),
             dma((narrow - 1,)), dma((narrow - 1,)),
-            dma((narrow - 1,)), dma((narrow - 1,)),
+            dma((narrow - 1, blocks)), dma((narrow - 1, blocks)),
             dma,
         ],
         compiler_params=pltpu.CompilerParams(

time: 99.1 us -> 101 us (1.019)
  Pallas kernels: 82.2 us -> 84.5 us
    pallas_call x1, Pallas kernels: 82.2 us -> 84.5 us  [per_device(): pl.pallas_call(functools.partial(kernel, wide, narrow), out_shape=(jax.Sh...]
where the time goes in v3:
time: 101 us; the launch traced here: 100 us
  Pallas kernels  84.5 us (84%)
  local copies, waits for them, and re-layouts  15.1 us (15%)
    pallas_call x1, Pallas kernels, per_device(): pl.pallas_call(functools.partial(kernel, wide, narrow), out_shape=(jax.Sh...  84.5 us
    unnamed x12, local copies, waits for them, and re-layouts  13 us
    slice x1, local copies, waits for them, and re-layouts, per_device(): window_factor[k, :, j, :]  2.11 us

profile of v3, /device:TPU:0, one launch (start us, length us, event | category | flops | bytes accessed | tf_op | source)
XLA Modules:
  0.0 100.4 jit_solution(13510764964632599738)
XLA Ops:
  0.6 2.1 %fusion.6 = (bf16[1,64,1,512]{3,2,1,0:T(2,128)(2,1)S(1)}, bf16[1,64,1,512]{3,2,1,0:T(2,128)(2,1)S(1)}, bf16[1,64,1,512]{3,2,1,0:T(2,128)(2,1)S(1)}, bf16[1,64,1,...) fusion(bf16[4,64,4,512]{3,2,1,0:T(4,128)(2,1)} %param.7), kind=kLoop, calls=%fused_computation.13 | loop fusion | bytes 786432 | tf_op jit(solution)/shard_map/slice | solution.py:391
  2.9 0.0 copy-start.1
  2.9 8.4 %copy.39 = bf16[2048,4,512]{2,0,1:T(8,128)(2,1)} copy(bf16[2048,4,512]{2,1,0:T(4,128)(2,1)} %param.9) | data formatting | bytes 16777216 | tf_op args[4]
  11.3 0.0 copy-done.1
  11.3 84.5 %shard_map.68 = (bf16[4,512,512]{2,1,0:T(8,128)(2,1)}, f32[1024,512]{1,0:T(8,128)}) custom-call(bf16[4,64,512]{2,1,0:T(8,128)(2,1)} %right.1, f32[1,4,64,512]{3,2,1,0:T(8,128)} %partial.1, bf16[6,64,512]{2,1,0:T(8,128)(2,1)} %copy-done.1, bf16[4,64,512]{2,1,0:T(8,128)(2,1)} %inverse.1, bf16[4,2048,512]{2,1,0:T(8,128)(2,1)} %bitcast.27), custom_call_target="tpu_custom_call" | custom-call | tf_op jit(solution)/shard_map/pallas_call | solution.py:405
  95.8 0.0 copy-start
  95.8 3.2 %copy.47 = bf16[4,512,512]{2,1,0:T(8,128)(2,1)} copy(bf16[4,512,512]{2,1,0:T(8,128)(2,1)} %get-tuple-element.10) | data formatting | bytes 4194304
  99.0 0.0 copy-done
  99.0 1.3 %copy.48 = f32[1024,512]{1,0:T(8,128)} copy(f32[1024,512]{1,0:T(8,128)S(1)} %copy-done) | data formatting | bytes 4194304
  (6 shorter events, 0.1 us)
Async XLA Ops:
  2.9 8.5 %copy-start.1 = (bf16[6,64,512]{2,1,0:T(8,128)(2,1)}, bf16[6,64,512]{2,1,0:T(8,128)(2,1)S(1)}, u32[]{:S(2)}) copy-start(bf16[6,64,512]{2,1,0:T(8,128)(2,1)S(1)} %fusion.window) | copy-start | bytes 1179652
  95.8 3.2 %copy-start = (f32[1024,512]{1,0:T(8,128)S(1)}, f32[1024,512]{1,0:T(8,128)}, u32[]{:S(2)}) copy-start(f32[1024,512]{1,0:T(8,128)} %get-tuple-element.11) | copy-start | bytes 6291460

commit v4 on v2

--- a/solution.py
+++ b/solution.py
@@ -209,12 +209,12 @@
     def t_copy(s, slot):
         to = place.side(s)
         return side_copy(
-            factor.at[:, pl.ds(pl.multiple_of(to * trail, trail), trail), :], tbuf.at[slot],
+            factor.at[pl.ds(pl.multiple_of(to * trail, trail), trail)], tbuf.at[slot],
             t_s.at[s - 1], t_r.at[s - 1], s,
         )
 
     t_here = pltpu.make_async_copy(
-        factor.at[:, pl.ds(pl.multiple_of(n * trail, trail), trail), :], tbuf.at[n], t_own
+        factor.at[pl.ds(pl.multiple_of(n * trail, trail), trail)], tbuf.at[n], t_own
     )
 
     for s in shifts:
@@ -294,7 +294,7 @@
             at = pl.ds(pl.multiple_of(t * high, high), high)
             total = None
             for h in range(narrow):
-                term = jnp.dot(tbuf[h, k, at, :], xbuf[k, h * cols:(h + 1) * cols, :], preferred_element_type=F32)
+                term = jnp.dot(tbuf[h, at, k, :], xbuf[k, h * cols:(h + 1) * cols, :], preferred_element_type=F32)
                 total = term if total is None else total + term
             if k == 0:
                 trailing[at, :] = total
@@ -371,7 +371,7 @@
     trail = trailing_factor.shape[0] // narrow
     outer = wide // INNER
     window = jnp.stack([window_factor[k, :, j, :] for k in range(blocks) for j in range(k)])
-    factor = jnp.transpose(trailing_factor, (1, 0, 2))
+    factor = trailing_factor
     dma = pltpu.SemaphoreType.DMA
 
     def gather_sems(peers):
@@ -396,7 +396,7 @@
             pltpu.VMEM((blocks, 2, outer, INNER, rows, rhs // 2), BF16),
             pltpu.VMEM((blocks, narrow, outer, INNER, rows, cols), BF16),
             pltpu.VMEM((blocks, step_rows, rhs), BF16),
-            pltpu.VMEM((narrow, blocks, trail, cols), BF16),
+            pltpu.VMEM((narrow, trail, blocks, cols), BF16),
             pltpu.VMEM((narrow - 1, blocks, rows, rhs), F32),
             pltpu.VMEM((narrow, blocks * (blocks - 1) // 2, rows, cols), BF16),
             pltpu.VMEM((rows, rhs), F32),

time: 99.1 us -> 101 us (1.019)
  Pallas kernels: 82.2 us -> 92.7 us
  local copies, waits for them, and re-layouts: 15.1 us -> 7.45 us
    pallas_call x1, Pallas kernels: 82.2 us -> 92.7 us  [per_device(): pl.pallas_call(functools.partial(kernel, wide, narrow), out_shape=(jax.Sh...]
    unnamed x12 -> x11, local copies, waits for them, and re-layouts: 13 us -> 5.32 us
where the time goes in v4:
time: 101 us
  Pallas kernels  92.7 us (92%)
  local copies, waits for them, and re-layouts  7.45 us (7%)
    pallas_call x1, Pallas kernels, per_device(): pl.pallas_call(functools.partial(kernel, wide, narrow), out_shape=(jax.Sh...  92.7 us
    unnamed x11, local copies, waits for them, and re-layouts  5.32 us
    slice x1, local copies, waits for them, and re-layouts, per_device(): window_factor[k, :, j, :]  2.11 us

profile of v4, /device:TPU:0, one launch (start us, length us, event | category | flops | bytes accessed | tf_op | source)
XLA Modules:
  0.0 100.8 jit_solution(10289876191703062898)
XLA Ops:
  0.6 2.1 %fusion.6 = (bf16[1,64,1,512]{3,2,1,0:T(2,128)(2,1)S(1)}, bf16[1,64,1,512]{3,2,1,0:T(2,128)(2,1)S(1)}, bf16[1,64,1,512]{3,2,1,0:T(2,128)(2,1)S(1)}, bf16[1,64,1,...) fusion(bf16[4,64,4,512]{3,2,1,0:T(4,128)(2,1)} %param.7), kind=kLoop, calls=%fused_computation.12 | loop fusion | bytes 786432 | tf_op jit(solution)/shard_map/slice | solution.py:373
  2.9 0.0 copy-start.1
  2.9 0.7 copy-done.1
  3.6 92.7 %shard_map.68 = (bf16[4,512,512]{2,1,0:T(8,128)(2,1)}, f32[1024,512]{1,0:T(8,128)}) custom-call(bf16[4,64,512]{2,1,0:T(8,128)(2,1)} %right.1, f32[1,4,64,512]{3,2,1,0:T(8,128)} %partial.1, bf16[6,64,512]{2,1,0:T(8,128)(2,1)} %copy-done.1, bf16[4,64,512]{2,1,0:T(8,128)(2,1)} %inverse.1, bf16[2048,4,512]{2,1,0:T(4,128)(2,1)} %factor.1), custom_call_target="tpu_custom_call" | custom-call | tf_op jit(solution)/shard_map/pallas_call | solution.py:387
  96.3 0.0 copy-start
  96.3 3.2 %copy.44 = bf16[4,512,512]{2,1,0:T(8,128)(2,1)} copy(bf16[4,512,512]{2,1,0:T(8,128)(2,1)} %get-tuple-element.10) | data formatting | bytes 4194304
  99.5 0.0 copy-done
  99.5 1.3 %copy.45 = f32[1024,512]{1,0:T(8,128)} copy(f32[1024,512]{1,0:T(8,128)S(1)} %copy-done) | data formatting | bytes 4194304
  (6 shorter events, 0.1 us)
Async XLA Ops:
  2.9 0.7 copy-start.1
  96.3 3.2 %copy-start = (f32[1024,512]{1,0:T(8,128)S(1)}, f32[1024,512]{1,0:T(8,128)}, u32[]{:S(2)}) copy-start(f32[1024,512]{1,0:T(8,128)} %get-tuple-element.11) | copy-start | bytes 6291460
